TPU v7x, 32 devices: a whole 2x2x4 slice. The times are simulated.
32 devices in a mesh: img: 4 (over x, core), txt: 4 (over z), rep: 2 (over y).
Axes of the slice: x: 2, y: 2, z: 4, core: 2. Of those that a mesh axis runs over, the one named last changes fastest.
Arguments:
- images: bfloat16 [5120, 1152], P(('img', 'txt', 'rep'))
- texts: bfloat16 [5120, 1152], P(('txt', 'rep', 'img'))
- partner: int32 [5120], replicated, may hold values from 0 to 5119, as said below
- log_scale: float32 [1], replicated, may hold values from 2 to 2.5
- bias: float32 [1], replicated, may hold values from -8 to -6
Outputs:
- grad_images: float32 [5120, 1152], P(('img', 'txt', 'rep'))
- grad_texts: float32 [5120, 1152], P(('txt', 'rep', 'img'))
- scalars: float32 [3], replicated
Inputs may be any that keep to these rules, and one draw needn't show every extreme that they name: partner[a] is the text row paired with image row a; every text row is named exactly once.
All inputs are finite; a program needn't handle non-finite values.
Results may differ from a plain program's by a relative error of at most 0.0039.
Values may be sent and summed in bfloat16 or wider, within the bound.
A program may use at most 128 MiB of HBM per device.

v0:
```python
import jax
import jax.numpy as jnp
from jax import lax
from jax.sharding import PartitionSpec as P


def unit_rows(values):
    full = values.astype(jnp.float32)
    norm = jnp.sqrt(jnp.sum(full * full, axis=1, keepdims=True) + 1e-06)
    return (full / norm, norm)


def on_device(images, texts, partner, log_scale, bias):
    rows = images.shape[0]
    n_img = lax.axis_size("img")
    n_txt = lax.axis_size("txt")
    n_rep = lax.axis_size("rep")
    i_index = lax.axis_index("img")
    j_index = lax.axis_index("txt")
    r_index = lax.axis_index("rep")
    block = rows * n_txt * n_rep
    img_unit, img_norm = unit_rows(images)
    txt_unit, txt_norm = unit_rows(texts)
    img_low = img_unit.astype(jnp.bfloat16)
    txt_low = txt_unit.astype(jnp.bfloat16)
    scale = jnp.exp(log_scale[0])
    shift = bias[0]
    img_block = lax.all_gather(img_low, ("txt", "rep"), axis=0, tiled=True)
    img_ids = i_index * block + jnp.arange(block, dtype=jnp.int32)
    img_partner = partner[img_ids]
    piece = lax.all_gather(txt_low, "img", axis=0, tiled=True)
    cols = piece.shape[0]
    ids = j_index * block + r_index * (rows * n_img) + jnp.arange(cols, dtype=jnp.int32)
    sims = lax.dot_general(
        img_block, piece, (((1,), (1,)), ((), ())), preferred_element_type=jnp.float32
    )
    logits = scale * sims + shift
    positive = img_partner[:, None] == ids[None, :]
    sign = jnp.where(positive, jnp.float32(1.0), jnp.float32(-1.0))
    margin = sign * logits
    pair_loss = jax.nn.softplus(-margin)
    slope = -sign * jax.nn.sigmoid(-margin)
    grad_tile = (scale * slope).astype(jnp.bfloat16)
    grad_img = jnp.dot(grad_tile, piece, preferred_element_type=jnp.float32)
    txt_piece = lax.dot_general(
        grad_tile, img_block, (((0,), (0,)), ((), ())), preferred_element_type=jnp.float32
    )
    grad_txt = txt_piece
    stats = jnp.stack([jnp.sum(pair_loss), jnp.sum(slope * scale * sims), jnp.sum(slope)])
    grad_img, grad_txt, stats = (grad_img, grad_txt, stats)
    img_own = lax.psum_scatter(grad_img, ("txt", "rep"), scatter_dimension=0, tiled=True)
    txt_mid = lax.psum_scatter(grad_txt, "img", scatter_dimension=0, tiled=True)
    totals = lax.psum(stats, ("img", "txt", "rep"))
    pair_total = rows * n_img * n_txt * n_rep
    scalars = totals / pair_total
    grad_images = (
        img_own - img_unit * jnp.sum(img_unit * img_own, axis=1, keepdims=True)
    ) / img_norm
    grad_texts = (
        txt_mid - txt_unit * jnp.sum(txt_unit * txt_mid, axis=1, keepdims=True)
    ) / txt_norm
    return (grad_images, grad_texts, scalars)


def solution(mesh):
    in_specs = (P(("img", "txt", "rep"), None), P(("txt", "rep", "img"), None), P(), P(), P())
    out_specs = (P(("img", "txt", "rep"), None), P(("txt", "rep", "img"), None), P())
    return jax.shard_map(
        on_device, mesh=mesh, in_specs=in_specs, out_specs=out_specs, check_vma=False
    )
```

profile of v0, /device:TPU:0, one launch (start us, length us, event | category | flops | bytes accessed | tf_op | source)
XLA Modules:
  0.0 269.8 jit_solution(10911858765793382675)
XLA Ops:
  7.2 0.0 copy-start
  7.2 0.0 all-gather.5.cloned.1.call-start
  7.2 1.1 fusion.3
  8.4 1.9 fusion.8
  10.2 0.0 all-gather.5.cloned.1.call-update
  10.3 0.0 all-gather.3.cloned.1.call-start
  10.3 1.1 fusion.2
  11.5 1.9 fusion.7
  13.3 0.0 all-gather.3.cloned.1.call-update
  13.4 0.0 reduce-scatter.5.cloned.1.call-start
  14.8 0.0 copy-done
  14.8 7.1 %gather_fusion = s32[1280]{0:T(1024)S(1)} fusion(s32[5120]{0:T(1024)S(1)} %copy-done, s32[2048]{0:T(1024)S(1)} %pad_clamp_fusion), kind=kCustom, calls=%fused_computation | custom fusion | bytes 15360 | tf_op jit(solution)/shard_map/gather | solution.py:30
  21.9 10.3 %all-gather.5.cloned.1.call-done = bf16[640,1152]{1,0:T(8,128)(2,1)} async-done(((bf16[160,1152]{1,0:T(8,128)(2,1)}), bf16[640,1152]{1,0:T(8,128)(2,1)}) %all-gather.5.cloned.1.call-update) | async-done | bytes 1474576 | tf_op jit(solution)/shard_map/all_gather | solution.py:31
  32.2 61.2 %all-gather.3.cloned.1.call-done = bf16[1280,1152]{1,0:T(8,128)(2,1)} async-done(((bf16[160,1152]{1,0:T(8,128)(2,1)}), bf16[1280,1152]{1,0:T(8,128)(2,1)}) %all-gather.3.cloned.1.call-update) | async-done | bytes 2949136 | tf_op jit(solution)/shard_map/all_gather | solution.py:28
  93.4 0.0 copy-start.3
  93.4 8.0 %fusion.1 = (f32[]{:T(128)}, f32[]{:T(128)}, f32[]{:T(128)}, f32[1280,640]{1,0:T(8,128)S(1)}) fusion(f32[]{:T(128)} %bitcast.10, s32[640]{0:T(1024)S(1)} %iota_add_fusion, f32[]{:T(128)} %bitcast, s32[1280]{0:T(1024)S(1)} %gather_fusion, bf16[1280,1152]{1,0:T(8,128)(2,1)} %all-gather.3.cloned.1.call-done, bf16[640,1152]{1,0:T(8,128)(2,1)} %all-gather.5.cloned.1.call-done), kind=kOutput, calls=%fused_computation.5 | convolution fusion | flops 1904640000 | bytes 7708180 | tf_op jit(solution)/shard_map/dot_general | solution.py:34
  101.4 0.0 copy-start.5
  101.4 1.8 copy-done.5
  103.2 0.0 copy-done.3
  103.2 0.0 copy-start.4
  103.2 4.5 %fusion.4 = f32[640,1152]{1,0:T(8,128)} fusion(bf16[1280,1152]{1,0:T(8,128)(2,1)S(1)} %copy-done.3, f32[]{:T(128)} %bitcast, f32[1280,640]{1,0:T(8,128)S(1)} %get-tuple-element.6, f32[]{:T(128)} %bitcast.11, s32[640]{0:T(1024)S(1)} %iota_add_fusion, s32[1280]{0:T(1024)S(1)} %gather_fusion), kind=kOutput, calls=%fused_computation.18 | convolution fusion | flops 1896448000 | bytes 9182728 | tf_op jit(solution)/shard_map/dot_general | solution.py:45
  107.7 0.0 reduce-scatter.5.cloned.1.call-update
  107.7 0.0 reduce-scatter.3.cloned.1.call-start
  107.8 0.0 copy-done.4
  107.8 8.2 %fusion.5 = f32[1280,1152]{1,0:T(8,128)} fusion(bf16[640,1152]{1,0:T(8,128)(2,1)S(1)} %copy-done.4, f32[]{:T(128)} %bitcast, f32[1280,640]{1,0:T(8,128)} %copy-done.5, f32[]{:T(128)} %bitcast.9, s32[640]{0:T(1024)S(1)} %iota_add_fusion, s32[1280]{0:T(1024)S(1)} %gather_fusion), kind=kOutput, calls=%fused_computation.19 | convolution fusion | flops 1896448000 | bytes 10657288 | tf_op jit(solution)/shard_map/dot_general | solution.py:44
  116.0 0.0 copy-start.1
  116.0 0.0 copy-start.2
  116.0 0.0 reduce-scatter.3.cloned.1.call-update
  116.0 2.1 pad_maximum_fusion
  118.1 39.5 %psum.7 = f32[3]{0:T(128)S(1)} all-reduce(f32[3]{0:T(128)S(1)} %pad_maximum_fusion), channel_id=1, replica_groups=mesh['img'=4,'txt'=4,'rep'=2] {'img','txt','rep'}, use_global_device_ids=true, to_apply=%region_9.10 | all-reduce | flops 3 | bytes 24 | tf_op jit(solution)/shard_map/psum | solution.py:53
  157.5 0.5 broadcast_multiply_fusion
  158.0 0.0 reduce-scatter.5.cloned.1.call-done
  158.0 0.0 copy-done.1
  158.0 1.4 multiply_reduce_fusion.1
  159.4 2.2 subtract_divide_fusion
  161.6 98.1 %reduce-scatter.3.cloned.1.call-done = f32[160,1152]{1,0:T(8,128)} async-done(((f32[1280,1152]{1,0:T(8,128)}), f32[160,1152]{1,0:T(8,128)}) %reduce-scatter.3.cloned.1.call-update) | async-done | bytes 737296 | tf_op jit(solution)/shard_map/reduce_scatter | solution.py:51
  259.7 0.0 copy-done.2
  259.7 1.4 multiply_reduce_fusion.2
  261.1 2.2 subtract_divide_fusion.1
  (5 shorter events, 0.1 us)
Async XLA Ops:
  7.2 7.6 %copy-start = (s32[5120]{0:T(1024)S(1)}, s32[5120]{0:T(1024)}, u32[]{:S(2)}) copy-start(s32[5120]{0:T(1024)} %param.7) | copy-start | bytes 61444
  7.2 25.1 %all-gather.5.cloned.1.call-start = ((), (), s32[]{:S(2)}) async-start(), calls=%async_computation.3 | async-start | bytes 1843200 | tf_op jit(solution)/shard_map/all_gather | solution.py:31
  10.3 83.1 %all-gather.3.cloned.1.call-start = ((), (), s32[]{:S(2)}) async-start(), calls=%async_computation.2 | async-start | bytes 3317760 | tf_op jit(solution)/shard_map/all_gather | solution.py:28
  13.4 144.7 %reduce-scatter.5.cloned.1.call-start = ((), (), s32[]{:S(2)}) async-start(), calls=%async_computation.5 | async-start | bytes 3686400 | tf_op jit(solution)/shard_map/reduce_scatter | solution.py:52
  93.4 9.8 %copy-start.3 = (bf16[1280,1152]{1,0:T(8,128)(2,1)S(1)}, bf16[1280,1152]{1,0:T(8,128)(2,1)}, u32[]{:S(2)}) copy-start(bf16[1280,1152]{1,0:T(8,128)(2,1)} %all-gather.3.cloned.1.call-done) | copy-start | bytes 8847364
  101.4 1.8 copy-start.5
  103.2 4.6 %copy-start.4 = (bf16[640,1152]{1,0:T(8,128)(2,1)S(1)}, bf16[640,1152]{1,0:T(8,128)(2,1)}, u32[]{:S(2)}) copy-start(bf16[640,1152]{1,0:T(8,128)(2,1)} %all-gather.5.cloned.1.call-done) | copy-start | bytes 4423684
  107.7 152.0 %reduce-scatter.3.cloned.1.call-start = ((), (), s32[]{:S(2)}) async-start(), calls=%async_computation.4 | async-start | bytes 6635520 | tf_op jit(solution)/shard_map/reduce_scatter | solution.py:51
  116.0 42.1 %copy-start.1 = (bf16[160,1152]{1,0:T(8,128)(2,1)S(1)}, bf16[160,1152]{1,0:T(8,128)(2,1)}, u32[]{:S(2)}) copy-start(bf16[160,1152]{1,0:T(8,128)(2,1)} %param.6) | copy-start | bytes 1105924
  116.0 143.8 %copy-start.2 = (bf16[160,1152]{1,0:T(8,128)(2,1)S(1)}, bf16[160,1152]{1,0:T(8,128)(2,1)}, u32[]{:S(2)}) copy-start(bf16[160,1152]{1,0:T(8,128)(2,1)} %param.5) | copy-start | bytes 1105924
Sparse Core Ops, SparseCore 0:
  10.4 21.7 all-gather.4
  35.0 58.3 all-gather.2
  107.8 35.6 reduce-scatter.4
  147.5 112.2 reduce-scatter.2
where the time goes:
time: 270 us
  waiting for transfers between devices  170 us (63%)
  blocking collectives  39.5 us (15%)
  matrix products  20.7 us (8%)
  other arithmetic  15.8 us (6%)
  between operations  15.2 us (6%)
  local copies, waits for them, and re-layouts  8.86 us (3%)
    reduce_scatter x1, waiting for transfers between devices, on_device(): lax.psum_scatter(grad_img, ('txt', 'rep'), scatter_dimension=0, tiled=True)  98.1 us
    all_gather x1, waiting for transfers between devices, on_device(): img_block = lax.all_gather(img_low, ('txt', 'rep'), axis=0, tiled=True)  61.2 us
    psum x1, blocking collectives, on_device(): totals = lax.psum(stats, ('img', 'txt', 'rep'))  39.5 us
    all_gather x1, waiting for transfers between devices, on_device(): piece = lax.all_gather(txt_low, 'img', axis=0, tiled=True)  10.3 us
    dot_general x1, matrix products, on_device(): grad_img = jnp.dot(grad_tile, piece, preferred_element_type=jnp.float32)  8.2 us
    dot_general x1, matrix products, on_device(): lax.dot_general(img_block, piece, (((1,), (1,)), ((), ())), preferred_ele...  8.02 us
    gather x1, local copies, waits for them, and re-layouts, on_device(): img_partner = partner[img_ids]  7.08 us
  transfers between devices with their start and end apart: 4, of which 3 were waited for; matrix products, arithmetic and copies ran while one was open for 9% of the time, Pallas kernels for 0%

commit v1 on v0

v1 whole, which is shorter than its diff:
```python
import functools

import jax
import jax.numpy as jnp
from jax import lax
from jax.experimental import pallas as pl
from jax.experimental.pallas import tpu as pltpu
from jax.sharding import PartitionSpec as P

MESH = pl.DeviceIdType.MESH
F32 = jnp.float32
BF16 = jnp.bfloat16
CHUNKS = 5


def row_norm(full):
    return jnp.sqrt(jnp.sum(full * full, axis=1, keepdims=True) + 1e-06)


def kernel(
    dims,
    images, texts, partner, log_scale, bias,
    out_img, out_txt, out_s,
    img_buf, txt_buf, gi, gt_own, gt_cs, gt_cr,
    gi_s1, gi_r1, gi_s2, gi_r2, gt_xs, gt_xr, gt_hs, gt_hr,
    stat_acc, st_buf,
    il_s, il_r, ir_s, ir_r, th_s, th_r, tx_s, tx_r, tc_s, tc_r,
    g1_s, g1_r, g2_s, g2_r, gc_s, gc_r, gx_s, gx_r, gh_s, gh_r, ss, sr,
):
    X, A, B, R = dims
    n_img, n_txt = 2 * X, A * B
    rows, width = images.shape
    crow = rows // CHUNKS
    i = lax.axis_index("img")
    t = lax.axis_index("txt")
    r = lax.axis_index("rep")
    x, c = i // 2, i % 2
    h, l = t // A, t % A
    other = 1 - c

    def rep_id(d):
        return {"rep": (r + d) % R}

    def lo_id(d):
        return {"txt": h * A + (l + d) % A}

    def hi_id(d):
        return {"txt": ((h + d) % B) * A + l}

    def x_id(d):
        return {"img": ((x + d) % X) * 2 + c}

    core_id = {"img": x * 2 + other}

    def signal(dev):
        pl.semaphore_signal(barrier, inc=1, device_id=dev, device_id_type=MESH)

    def copy(src, dst, send, recv, dev):
        return pltpu.make_async_remote_copy(
            src_ref=src, dst_ref=dst, send_sem=send, recv_sem=recv,
            device_id=dev, device_id_type=MESH,
        )

    barrier = pltpu.get_barrier_semaphore()
    peers = (
        [rep_id(d) for d in range(1, R)] + [lo_id(d) for d in range(1, A)]
        + [hi_id(d) for d in range(1, B)] + [x_id(d) for d in range(1, X)] + [core_id]
    )
    for dev in peers:
        signal(dev)

    def img_at(lp, rp, ch):
        return img_buf.at[pl.ds(pl.multiple_of((lp * R + rp) * rows + ch * crow, 16), crow)]

    def txt_at(hp, xp, cp, ch):
        return txt_buf.at[
            pl.ds(pl.multiple_of(((hp * X + xp) * 2 + cp) * rows + ch * crow, 16), crow)
        ]

    def img_lo(d, ch):
        return copy(img_at(l, r, ch), img_at(l, r, ch), il_s.at[d, ch], il_r.at[d, ch], lo_id(d))

    def img_rep(dl, d, ch):
        lp = (l + dl) % A
        ref = img_at(lp, r, ch)
        return copy(ref, ref, ir_s.at[dl, d, ch], ir_r.at[dl, d, ch], rep_id(d))

    def txt_hi(d, ch):
        ref = txt_at(h, x, c, ch)
        return copy(ref, ref, th_s.at[d, ch], th_r.at[d, ch], hi_id(d))

    def txt_x(dh, d, ch):
        ref = txt_at((h + dh) % B, x, c, ch)
        return copy(ref, ref, tx_s.at[dh, d, ch], tx_r.at[dh, d, ch], x_id(d))

    def txt_core(dh, dx, ch):
        ref = txt_at((h + dh) % B, (x + dx) % X, c, ch)
        return copy(ref, ref, tc_s.at[dh, dx, ch], tc_r.at[dh, dx, ch], core_id)

    full = images[...].astype(F32)
    img_norm = row_norm(full)
    img_buf[pl.ds(pl.multiple_of((l * R + r) * rows, 16), rows)] = (full / img_norm).astype(BF16)
    pl.semaphore_wait(barrier, len(peers))
    for ch in range(CHUNKS):
        for d in range(1, A):
            img_lo(d, ch).start()
        for d in range(1, R):
            img_rep(0, d, ch).start()
    full = texts[...].astype(F32)
    txt_norm = row_norm(full)
    txt_buf[pl.ds(pl.multiple_of(((h * X + x) * 2 + c) * rows, 16), rows)] = (
        full / txt_norm
    ).astype(BF16)
    for ch in range(CHUNKS):
        for d in range(1, B):
            txt_hi(d, ch).start()
        for d in range(1, X):
            txt_x(0, d, ch).start()
        txt_core(0, 0, ch).start()

    gi[...] = jnp.zeros_like(gi)
    stat_acc[...] = jnp.zeros_like(stat_acc)

    for ch in range(CHUNKS):
        for d in range(1, A):
            img_lo(d, ch).wait_recv()
            for e in range(1, R):
                img_rep(A - d, e, ch).start()
        for d in range(1, B):
            txt_hi(d, ch).wait_recv()
            for e in range(1, X):
                txt_x(B - d, e, ch).start()
            txt_core(B - d, 0, ch).start()
        for d in range(1, X):
            txt_x(0, d, ch).wait_recv()
            txt_core(0, X - d, ch).start()
    for ch in range(CHUNKS):
        for dh in range(1, B):
            for d in range(1, X):
                txt_x(dh, d, ch).wait_recv()
                txt_core(dh, X - d, ch).start()
    for ch in range(CHUNKS):
        for dl in range(A):
            for d in range(1, R):
                img_rep(dl, d, ch).wait_recv()

    scale = jnp.exp(jnp.full((8, 128), log_scale[0], F32))[:1, :1]
    shift = bias[0]
    group = A * R * rows
    lanes = group // 128
    first = (i * n_txt + h * A) * R * rows // 128
    wanted = [partner[pl.ds(first + k, 1), :] for k in range(lanes)]
    wanted = jnp.concatenate(wanted, axis=1)

    def grad_core(k):
        return copy(gt_cs.at[k], gt_cr.at[k], gc_s.at[k], gc_r.at[k], core_id)

    def grad_x(dx, dh, ch):
        part = pl.ds(pl.multiple_of(ch * crow, 16), crow)
        return copy(
            gt_xs.at[dx - 1, dh, part], gt_xr.at[dx - 1, dh, part],
            gx_s.at[dx - 1, dh, ch], gx_r.at[dx - 1, dh, ch], x_id(dx),
        )

    def finish(k):
        grad_core(k).wait_recv()
        dx = X - 1 - k // B
        dh = B - 1 - k % B

        @pl.when(dx > 0)
        def _():
            gt_xs[dx - 1, dh] = (gt_own[k] + gt_cr[k]).astype(BF16)
            for ch in range(CHUNKS):
                grad_x(dx, dh, ch).start()

    def step(k, _):
        dx = X - 1 - k // B
        dh = B - 1 - k % B
        hp, xp = (h + dh) % B, (x + dx) % X
        for ch in range(CHUNKS):
            txt_core(dh, dx, ch).wait_recv()
        base = pl.multiple_of((hp * X + xp) * 2 * rows, 16)
        block = txt_buf[pl.ds(base, 2 * rows)]
        all_img = img_buf[...]
        sims = lax.dot_general(
            block, all_img, (((1,), (1,)), ((), ())), preferred_element_type=F32
        )
        start = ((hp * A + l) * R + r) * n_img * rows + xp * 2 * rows
        ids = start + lax.broadcasted_iota(jnp.int32, sims.shape, 0)
        positive = ids == wanted
        scaled = scale * sims
        logits = scaled + shift
        margin = jnp.where(positive, logits, -logits)
        e = jnp.exp(-jnp.abs(margin))
        u = 1.0 + e
        inv = 1.0 / u
        loss = jnp.maximum(-margin, 0.0) + (jnp.log(u) + (e - (u - 1.0)) * inv)
        sig = jnp.where(margin >= 0.0, e, 1.0) * inv
        slope = jnp.where(positive, -sig, sig)
        grad = (scale * slope).astype(BF16)
        stat_acc[0:1, :] += jnp.sum(loss, axis=0, keepdims=True)
        stat_acc[1:2, :] += jnp.sum(slope * scaled, axis=0, keepdims=True)
        stat_acc[2:3, :] += jnp.sum(slope, axis=0, keepdims=True)
        g_txt = jnp.dot(grad, all_img, preferred_element_type=F32)
        mine = c == 0
        gt_cs[k] = jnp.where(mine, g_txt[rows:], g_txt[:rows])
        grad_core(k).start()
        gt_own[k] = jnp.where(mine, g_txt[:rows], g_txt[rows:])
        gi[...] += lax.dot_general(
            grad, block, (((0,), (0,)), ((), ())), preferred_element_type=F32
        )

        @pl.when(k > 0)
        def _():
            finish(k - 1)

        return 0

    lax.fori_loop(0, B * X, step, 0)

    def gi_at(dl, d, ch):
        lp, rp = (l + dl) % A, (r + d) % R
        return pl.ds(pl.multiple_of((lp * R + rp) * rows + ch * crow, 16), crow)

    def cut(ch):
        return pl.ds(ch * crow, crow)

    def grad_rep(d, dl, ch):
        return copy(
            gi_s1.at[d - 1, dl, cut(ch)], gi_r1.at[d - 1, dl, cut(ch)],
            g1_s.at[d - 1, dl, ch], g1_r.at[d - 1, dl, ch], rep_id(d),
        )

    def grad_lo(d, ch):
        return copy(
            gi_s2.at[d - 1, cut(ch)], gi_r2.at[d - 1, cut(ch)],
            g2_s.at[d - 1, ch], g2_r.at[d - 1, ch], lo_id(d),
        )

    def grad_hi(d, ch):
        return copy(
            gt_hs.at[d - 1, cut(ch)], gt_hr.at[d - 1, cut(ch)],
            gh_s.at[d - 1, ch], gh_r.at[d - 1, ch], hi_id(d),
        )

    for dl in list(range(1, A)) + [0]:
        for d in range(1, R):
            for ch in range(CHUNKS):
                gi_s1[d - 1, dl, cut(ch)] = gi[gi_at(dl, d, ch)].astype(BF16)
                grad_rep(d, dl, ch).start()
    finish(B * X - 1)

    st_axes = [
        (2, c, lambda d: core_id), (X, x, x_id), (R, r, rep_id), (B, h, hi_id), (A, l, lo_id),
    ]
    value = stat_acc[:, 0:128]
    for k in range(1, lanes):
        value = value + stat_acc[:, k * 128:(k + 1) * 128]

    def stat_copy(stage, d):
        size, at, ident = st_axes[stage]
        return copy(
            st_buf.at[stage, at], st_buf.at[stage, at], ss.at[stage, d], sr.at[stage, d], ident(d)
        )

    def stat_start(stage, value):
        st_buf[stage, st_axes[stage][1]] = value
        for d in range(1, st_axes[stage][0]):
            stat_copy(stage, d).start()

    def stat_end(stage):
        size = st_axes[stage][0]
        for d in range(1, size):
            stat_copy(stage, d).wait_recv()
        total = st_buf[stage, 0]
        for k in range(1, size):
            total = total + st_buf[stage, k]
        return total

    stat_start(0, value)
    value = stat_end(0)
    stat_start(1, value)

    def own_txt(dh, ch):
        k = B * (X - 1) + (B - 1 - dh)
        return gt_own[k, cut(ch)] + gt_cr[k, cut(ch)]

    for ch in range(CHUNKS):
        for dh in range(1, B):
            total = own_txt(dh, ch)
            for d in range(1, X):
                grad_x(d, dh, ch).wait_recv()
                total = total + gt_xr[d - 1, dh, cut(ch)].astype(F32)
            gt_hs[dh - 1, cut(ch)] = total.astype(BF16)
            grad_hi(dh, ch).start()
        for dl in range(1, A):
            total = gi[gi_at(dl, 0, ch)]
            for d in range(1, R):
                grad_rep(d, dl, ch).wait_recv()
                total = total + gi_r1[d - 1, dl, cut(ch)].astype(F32)
            gi_s2[dl - 1, cut(ch)] = total.astype(BF16)
            grad_lo(dl, ch).start()

    for stage in range(1, 4):
        value = stat_end(stage)
        stat_start(stage + 1, value)

    for ch in range(CHUNKS):
        part = cut(ch)
        total = own_txt(0, ch)
        for d in range(1, X):
            grad_x(d, 0, ch).wait_recv()
            total = total + gt_xr[d - 1, 0, part].astype(F32)
        for d in range(1, B):
            grad_hi(d, ch).wait_recv()
            total = total + gt_hr[d - 1, part].astype(F32)
        norm = txt_norm[ch * crow:(ch + 1) * crow]
        unit = texts[part].astype(F32) / norm
        along = jnp.sum(unit * total, axis=1, keepdims=True)
        out_txt[part] = (total - unit * along) / norm

        total = gi[gi_at(0, 0, ch)]
        for d in range(1, R):
            grad_rep(d, 0, ch).wait_recv()
            total = total + gi_r1[d - 1, 0, part].astype(F32)
        for d in range(1, A):
            grad_lo(d, ch).wait_recv()
            total = total + gi_r2[d - 1, part].astype(F32)
        norm = img_norm[ch * crow:(ch + 1) * crow]
        unit = images[part].astype(F32) / norm
        along = jnp.sum(unit * total, axis=1, keepdims=True)
        out_img[part] = (total - unit * along) / norm

    value = stat_end(4)
    pairs = rows * n_img * n_txt * R
    for k in range(3):
        out_s[k] = jnp.sum(value[k:k + 1, :]) / pairs

    for ch in range(CHUNKS):
        for d in range(1, A):
            img_lo(d, ch).wait_send()
            grad_lo(d, ch).wait_send()
        for d in range(1, R):
            for dl in range(A):
                img_rep(dl, d, ch).wait_send()
                grad_rep(d, dl, ch).wait_send()
        for d in range(1, B):
            txt_hi(d, ch).wait_send()
            grad_hi(d, ch).wait_send()
        for dh in range(B):
            for d in range(1, X):
                txt_x(dh, d, ch).wait_send()
                grad_x(d, dh, ch).wait_send()
            for dx in range(X):
                txt_core(dh, dx, ch).wait_send()
    for k in range(B * X):
        grad_core(k).wait_send()
    for stage in range(5):
        for d in range(1, st_axes[stage][0]):
            stat_copy(stage, d).wait_send()


def on_device(dims, images, texts, partner, log_scale, bias):
    X, A, B, R = dims
    rows, width = images.shape
    group = A * R * rows
    nt = B * X
    most = max(2, X, A, B, R)
    dma = pltpu.SemaphoreType.DMA
    vm = pl.BlockSpec(memory_space=pltpu.VMEM)
    sm = pl.BlockSpec(memory_space=pltpu.SMEM)
    C = CHUNKS
    return pl.pallas_call(
        functools.partial(kernel, dims),
        out_shape=(
            jax.ShapeDtypeStruct((rows, width), F32),
            jax.ShapeDtypeStruct((rows, width), F32),
            jax.ShapeDtypeStruct((3,), F32),
        ),
        in_specs=[vm, vm, vm, sm, sm],
        out_specs=(vm, vm, sm),
        scratch_shapes=[
            pltpu.VMEM((group, width), BF16),
            pltpu.VMEM((nt * 2 * rows, width), BF16),
            pltpu.VMEM((group, width), F32),
            pltpu.VMEM((nt, rows, width), F32),
            pltpu.VMEM((nt, rows, width), F32),
            pltpu.VMEM((nt, rows, width), F32),
            pltpu.VMEM((R - 1, A, rows, width), BF16),
            pltpu.VMEM((R - 1, A, rows, width), BF16),
            pltpu.VMEM((A - 1, rows, width), BF16),
            pltpu.VMEM((A - 1, rows, width), BF16),
            pltpu.VMEM((X - 1, B, rows, width), BF16),
            pltpu.VMEM((X - 1, B, rows, width), BF16),
            pltpu.VMEM((B - 1, rows, width), BF16),
            pltpu.VMEM((B - 1, rows, width), BF16),
            pltpu.VMEM((8, group), F32),
            pltpu.VMEM((5, most, 8, 128), F32),
            dma((A, C)), dma((A, C)), dma((A, R, C)), dma((A, R, C)),
            dma((B, C)), dma((B, C)), dma((B, X, C)), dma((B, X, C)),
            dma((B, X, C)), dma((B, X, C)),
            dma((R - 1, A, C)), dma((R - 1, A, C)), dma((A - 1, C)), dma((A - 1, C)),
            dma((nt,)), dma((nt,)),
            dma((X - 1, B, C)), dma((X - 1, B, C)), dma((B - 1, C)), dma((B - 1, C)),
            dma((5, most)), dma((5, most)),
        ],
        compiler_params=pltpu.CompilerParams(
            collective_id=0, has_side_effects=True, vmem_limit_bytes=60 * 2**20
        ),
    )(images, texts, partner.reshape(-1, 128), log_scale, bias)


def solution(mesh):
    n_img, n_txt, n_rep = mesh.shape["img"], mesh.shape["txt"], mesh.shape["rep"]
    dims = (n_img // 2, n_txt // 2, 2, n_rep)
    in_specs = (P(("img", "txt", "rep"), None), P(("txt", "rep", "img"), None), P(), P(), P())
    out_specs = (P(("img", "txt", "rep"), None), P(("txt", "rep", "img"), None), P())
    return jax.shard_map(
        functools.partial(on_device, dims), mesh=mesh,
        in_specs=in_specs, out_specs=out_specs, check_vma=False,
    )
```

time: 270 us -> 72.9 us (0.27)
  waiting for transfers between devices: 170 us -> 0 us
  Pallas kernels: 0 us -> 67.3 us
  blocking collectives: 39.5 us -> 0 us
  matrix products: 20.7 us -> 0 us
  other arithmetic: 15.8 us -> 0 us
  between operations: 15.2 us -> 1.94 us
  local copies, waits for them, and re-layouts: 8.86 us -> 3.48 us
    reduce_scatter x2 -> x0, waiting for transfers between devices: 98.1 us -> none  [the longest x1 98.1 us: on_device(): lax.psum_scatter(grad_img, ('txt', 'rep'), scatter_dimension=0, tiled=True)]
    all_gather x2 -> x0, waiting for transfers between devices: 71.5 us -> none  [the longest x1 61.2 us: on_device(): img_block = lax.all_gather(img_low, ('txt', 'rep'), axis=0, tiled=True)]
    pallas_call x0 -> x1, Pallas kernels: none -> 67.3 us  [on_device(): pl.pallas_call(functools.partial(kernel, dims), out_shape=(jax.ShapeDtype...]
    psum x1 -> x0, blocking collectives: 39.5 us -> none  [on_device(): totals = lax.psum(stats, ('img', 'txt', 'rep'))]
    dot_general x3 -> x0, matrix products: 20.7 us -> none  [the longest x1 8.2 us: on_device(): grad_img = jnp.dot(grad_tile, piece, preferred_element_type=jnp.float32)]
    gather x1 -> x0, local copies, waits for them, and re-layouts: 7.08 us -> none  [on_device(): img_partner = partner[img_ids]]
    reduce_sum x4 -> x0, other arithmetic: 5.02 us -> none  [the longest x2 2.29 us: unit_rows(): norm = jnp.sqrt(jnp.sum(full * full, axis=1, keepdims=True) + 1e-06)]
    div x3 -> x0, other arithmetic: 4.92 us -> none  [the longest x1 2.2 us: on_device(): (img_own - img_unit * jnp.sum(img_unit * img_own, axis=1, keepdims=True))...]
  transfers between devices with their start and end apart: 4 -> 0, of which waited for: 3 -> 0; matrix products, arithmetic and copies ran while one was open for 9% -> 0% of each run, Pallas kernels for 0% -> 0%
where the time goes in v1:
time: 72.9 us; the launch traced here: 72.8 us
  Pallas kernels  67.3 us (92%)
  local copies, waits for them, and re-layouts  3.48 us (5%)
  between operations  1.94 us (3%)
    pallas_call x1, Pallas kernels, on_device(): pl.pallas_call(functools.partial(kernel, dims), out_shape=(jax.ShapeDtype...  67.3 us
    unnamed x7, local copies, waits for them, and re-layouts  3.48 us

profile of v1, /device:TPU:0, one launch (start us, length us, event | category | flops | bytes accessed | tf_op | source)
XLA Modules:
  0.0 72.8 jit_solution(7485195812062214459)
XLA Ops:
  1.9 67.3 %shard_map.76 = (f32[160,1152]{1,0:T(8,128)}, f32[160,1152]{1,0:T(8,128)}, f32[3]{0:T(128)}) custom-call(bf16[160,1152]{1,0:T(8,128)(2,1)} %images.1, bf16[160,1152]{1,0:T(8,128)(2,1)} %texts.1, s32[40,128]{1,0:T(8,128)} %bitcast.1, f32[1]{0:T(128)S(6)} %copy.11.log_scale, f32[1]{0:T(128)S(6)} %copy.12.bias), custom_call_target="tpu_custom_call" | custom-call | tf_op jit(solution)/shard_map/pallas_call | solution.py:373
  69.3 0.0 copy-start
  69.3 2.1 %copy.13 = f32[160,1152]{1,0:T(8,128)} copy(f32[160,1152]{1,0:T(8,128)} %get-tuple-element.6) | data formatting | bytes 1474560
  71.4 0.0 copy-done
  71.4 0.0 copy-start.1
  71.4 0.9 %copy.14 = f32[160,1152]{1,0:T(8,128)} copy(f32[160,1152]{1,0:T(8,128)S(1)} %copy-done) | data formatting | bytes 1474560
  72.2 0.0 copy-done.1
  72.2 0.5 copy.15
Async XLA Ops:
  69.3 2.1 %copy-start = (f32[160,1152]{1,0:T(8,128)S(1)}, f32[160,1152]{1,0:T(8,128)}, u32[]{:S(2)}) copy-start(f32[160,1152]{1,0:T(8,128)} %get-tuple-element.7) | copy-start | bytes 2211844
  71.4 0.9 %copy-start.1 = (f32[3]{0:T(128)S(1)}, f32[3]{0:T(128)}, u32[]{:S(2)}) copy-start(f32[3]{0:T(128)} %get-tuple-element.8) | copy-start | bytes 40

commit v2 on v1

--- a/solution.py
+++ b/solution.py
@@ -50,6 +50,12 @@
     def x_id(d):
         return {"img": ((x + d) % X) * 2 + c}
 
+    def img_id(d):
+        return {"img": (i + d) % n_img}
+
+    def txt_id(d):
+        return {"txt": (t + d) % n_txt}
+
     core_id = {"img": x * 2 + other}
 
     def signal(dev):
@@ -63,8 +69,8 @@
 
     barrier = pltpu.get_barrier_semaphore()
     peers = (
-        [rep_id(d) for d in range(1, R)] + [lo_id(d) for d in range(1, A)]
-        + [hi_id(d) for d in range(1, B)] + [x_id(d) for d in range(1, X)] + [core_id]
+        [rep_id(d) for d in range(1, R)] + [img_id(d) for d in range(1, n_img)]
+        + [txt_id(d) for d in range(1, n_txt)]
     )
     for dev in peers:
         signal(dev)
@@ -243,19 +249,7 @@
             gh_s.at[d - 1, ch], gh_r.at[d - 1, ch], hi_id(d),
         )
 
-    for dl in list(range(1, A)) + [0]:
-        for d in range(1, R):
-            for ch in range(CHUNKS):
-                gi_s1[d - 1, dl, cut(ch)] = gi[gi_at(dl, d, ch)].astype(BF16)
-                grad_rep(d, dl, ch).start()
-    finish(B * X - 1)
-
-    st_axes = [
-        (2, c, lambda d: core_id), (X, x, x_id), (R, r, rep_id), (B, h, hi_id), (A, l, lo_id),
-    ]
-    value = stat_acc[:, 0:128]
-    for k in range(1, lanes):
-        value = value + stat_acc[:, k * 128:(k + 1) * 128]
+    st_axes = [(R, r, rep_id), (n_txt, t, txt_id), (n_img, i, img_id)]
 
     def stat_copy(stage, d):
         size, at, ident = st_axes[stage]
@@ -277,9 +271,18 @@
             total = total + st_buf[stage, k]
         return total
 
+    value = stat_acc[:, 0:128]
+    for k in range(1, lanes):
+        value = value + stat_acc[:, k * 128:(k + 1) * 128]
     stat_start(0, value)
-    value = stat_end(0)
-    stat_start(1, value)
+
+    for dl in list(range(1, A)) + [0]:
+        for d in range(1, R):
+            for ch in range(CHUNKS):
+                gi_s1[d - 1, dl, cut(ch)] = gi[gi_at(dl, d, ch)].astype(BF16)
+                grad_rep(d, dl, ch).start()
+    finish(B * X - 1)
+    stat_start(1, stat_end(0))
 
     def own_txt(dh, ch):
         k = B * (X - 1) + (B - 1 - dh)
@@ -301,9 +304,7 @@
             gi_s2[dl - 1, cut(ch)] = total.astype(BF16)
             grad_lo(dl, ch).start()
 
-    for stage in range(1, 4):
-        value = stat_end(stage)
-        stat_start(stage + 1, value)
+    stat_start(2, stat_end(1))
 
     for ch in range(CHUNKS):
         part = cut(ch)
@@ -331,7 +332,7 @@
         along = jnp.sum(unit * total, axis=1, keepdims=True)
         out_img[part] = (total - unit * along) / norm
 
-    value = stat_end(4)
+    value = stat_end(2)
     pairs = rows * n_img * n_txt * R
     for k in range(3):
         out_s[k] = jnp.sum(value[k:k + 1, :]) / pairs
@@ -355,7 +356,7 @@
                 txt_core(dh, dx, ch).wait_send()
     for k in range(B * X):
         grad_core(k).wait_send()
-    for stage in range(5):
+    for stage in range(3):
         for d in range(1, st_axes[stage][0]):
             stat_copy(stage, d).wait_send()
 
@@ -365,7 +366,7 @@
     rows, width = images.shape
     group = A * R * rows
     nt = B * X
-    most = max(2, X, A, B, R)
+    most = max(2 * X, A * B, R)
     dma = pltpu.SemaphoreType.DMA
     vm = pl.BlockSpec(memory_space=pltpu.VMEM)
     sm = pl.BlockSpec(memory_space=pltpu.SMEM)
@@ -395,14 +396,14 @@
             pltpu.VMEM((B - 1, rows, width), BF16),
             pltpu.VMEM((B - 1, rows, width), BF16),
             pltpu.VMEM((8, group), F32),
-            pltpu.VMEM((5, most, 8, 128), F32),
+            pltpu.VMEM((3, most, 8, 128), F32),
             dma((A, C)), dma((A, C)), dma((A, R, C)), dma((A, R, C)),
             dma((B, C)), dma((B, C)), dma((B, X, C)), dma((B, X, C)),
             dma((B, X, C)), dma((B, X, C)),
             dma((R - 1, A, C)), dma((R - 1, A, C)), dma((A - 1, C)), dma((A - 1, C)),
             dma((nt,)), dma((nt,)),
             dma((X - 1, B, C)), dma((X - 1, B, C)), dma((B - 1, C)), dma((B - 1, C)),
-            dma((5, most)), dma((5, most)),
+            dma((3, most)), dma((3, most)),
         ],
         compiler_params=pltpu.CompilerParams(
             collective_id=0, has_side_effects=True, vmem_limit_bytes=60 * 2**20

time: 72.9 us -> 71.5 us (0.981)
  Pallas kernels: 67.3 us -> 65.9 us
    pallas_call x1, Pallas kernels: 67.3 us -> 65.9 us  [on_device(): pl.pallas_call(functools.partial(kernel, dims), out_shape=(jax.ShapeDtype...]
where the time goes in v2:
time: 71.5 us; the launch traced here: 71.4 us
  Pallas kernels  65.9 us (92%)
  local copies, waits for them, and re-layouts  3.48 us (5%)
  between operations  1.94 us (3%)
    pallas_call x1, Pallas kernels, on_device(): pl.pallas_call(functools.partial(kernel, dims), out_shape=(jax.ShapeDtype...  65.9 us
    unnamed x7, local copies, waits for them, and re-layouts  3.48 us

profile of v2, /device:TPU:0, one launch (start us, length us, event | category | flops | bytes accessed | tf_op | source)
XLA Modules:
  0.0 71.4 jit_solution(2806790150811282839)
XLA Ops:
  1.9 65.9 %shard_map.76 = (f32[160,1152]{1,0:T(8,128)}, f32[160,1152]{1,0:T(8,128)}, f32[3]{0:T(128)}) custom-call(bf16[160,1152]{1,0:T(8,128)(2,1)} %images.1, bf16[160,1152]{1,0:T(8,128)(2,1)} %texts.1, s32[40,128]{1,0:T(8,128)} %bitcast.1, f32[1]{0:T(128)S(6)} %copy.11.log_scale, f32[1]{0:T(128)S(6)} %copy.12.bias), custom_call_target="tpu_custom_call" | custom-call | tf_op jit(solution)/shard_map/pallas_call | solution.py:374
  67.9 0.0 copy-start
  67.9 2.1 %copy.13 = f32[160,1152]{1,0:T(8,128)} copy(f32[160,1152]{1,0:T(8,128)} %get-tuple-element.6) | data formatting | bytes 1474560
  70.0 0.0 copy-done
  70.0 0.0 copy-start.1
  70.0 0.9 %copy.14 = f32[160,1152]{1,0:T(8,128)} copy(f32[160,1152]{1,0:T(8,128)S(1)} %copy-done) | data formatting | bytes 1474560
  70.8 0.0 copy-done.1
  70.8 0.5 copy.15
Async XLA Ops:
  67.9 2.1 %copy-start = (f32[160,1152]{1,0:T(8,128)S(1)}, f32[160,1152]{1,0:T(8,128)}, u32[]{:S(2)}) copy-start(f32[160,1152]{1,0:T(8,128)} %get-tuple-element.7) | copy-start | bytes 2211844
  70.0 0.9 %copy-start.1 = (f32[3]{0:T(128)S(1)}, f32[3]{0:T(128)}, u32[]{:S(2)}) copy-start(f32[3]{0:T(128)} %get-tuple-element.8) | copy-start | bytes 40
